TPU v7x, 128 devices: a whole 4x4x4 slice. The times are simulated.
128 devices in a mesh: seq: 32 (over z, x, core), ret: 4 (over y).
Axes of the slice: x: 4, y: 4, z: 4, core: 2. Of those that a mesh axis runs over, the one named last changes fastest.
Arguments:
- activations: bfloat16 [16384, 4096], P('seq'), may hold values from -6 to 6
- grad_out: bfloat16 [16384, 4096], P('seq'), may hold values from -6 to 6
- database: bfloat16 [1024, 128, 896], P(('seq', 'ret')), may hold values from -6 to 6
- owners: int32 [256, 2], P('seq'), may hold values from 0 to 3, all different within a row; in each aligned block of 8 rows (0 to 7, 8 to 15, ...) at most 5 rows name the same one
- row_index: int32 [256, 2], P('seq'), may hold values from 0 to 7
- w_cond: bfloat16 [2, 4096, 896], P(None, 'seq', 'ret'), may hold values from -0.09375 to 0.09375
- w_enc: bfloat16 [2, 896, 896], replicated, may hold values from -0.1875 to 0.1875
- w_query: bfloat16 [4096, 2048], P('seq', 'ret'), may hold values from -0.09375 to 0.09375
- w_kv: bfloat16 [2, 896, 2048], P(None, 'seq', 'ret'), may hold values from -0.1875 to 0.1875
- w_out: bfloat16 [2048, 4096], P('ret', 'seq'), may hold values from -0.125 to 0.125
Outputs:
- grad_x: bfloat16 [16384, 4096], P('seq', 'ret')
- grad_db: bfloat16 [1024, 128, 896], P(('seq', 'ret'))
- grad_wq: bfloat16 [4096, 2048], P('seq', 'ret')
- grad_wcond: bfloat16 [2, 4096, 896], P(None, 'seq', 'ret')
Inputs may be any that keep to these rules, and one draw needn't show every extreme that they name: The 2 neighbours of a stretch come from different owners. Among the 8 stretches of one index of seq, at most 5 neighbours come from one owner, and some index reaches 5.
All inputs are finite; a program needn't handle non-finite values.
Results may differ from a plain program's by a relative error of at most 0.035.
Values may be sent and summed in bfloat16 or wider, within the bound.
No kernel may reach another device: no remote copies, remote signals or barrier semaphores. Data moves between devices by JAX's collectives and lax.ppermute only.
A program may use at most 128 MiB of HBM per device.

v0:
```python
import jax
import jax.numpy as jnp
from jax import lax
from jax.sharding import PartitionSpec as P

HD = 128
ENC_HD = 128


def passed_along(value, axis, steps):
    count = lax.axis_size(axis)
    first, last = (max(0, -steps), min(count, count - steps))
    return lax.ppermute(value, axis, [(source, source + steps) for source in range(first, last)])


def project(left_op, right_op):
    return lax.dot_general(
        left_op,
        right_op,
        (((left_op.ndim - 1,), (0,)), ((), ())),
        preferred_element_type=jnp.float32,
    )


def project_back(left_op, right_op):
    return lax.dot_general(
        left_op,
        right_op,
        (((left_op.ndim - 1,), (1,)), ((), ())),
        preferred_element_type=jnp.float32,
    )


def encode_rows(neighbour_rows, cond_pairs, w_enc):
    item_count, row_length, enc_width = neighbour_rows.shape
    head_count = enc_width // ENC_HD
    score_scale = ENC_HD ** (-0.5)
    enc_queries = project(neighbour_rows, w_enc[0]).astype(jnp.bfloat16)
    q_heads = enc_queries.reshape(item_count, row_length, head_count, ENC_HD)
    k_heads = cond_pairs[:, :, 0].reshape(item_count, -1, head_count, ENC_HD)
    v_heads = cond_pairs[:, :, 1].reshape(item_count, -1, head_count, ENC_HD)
    scores = (
        jnp.einsum("nthd,nshd->nhts", q_heads, k_heads, preferred_element_type=jnp.float32)
        * score_scale
    )
    exponent = jnp.exp(scores)
    attn_probs = exponent / jnp.sum(exponent, axis=-1, keepdims=True)
    probs_low = attn_probs.astype(jnp.bfloat16)
    mixture = jnp.einsum("nhts,nshd->nthd", probs_low, v_heads, preferred_element_type=jnp.float32)
    mixture = mixture.reshape(item_count, row_length, enc_width).astype(jnp.bfloat16)
    encoded = (neighbour_rows.astype(jnp.float32) + project(mixture, w_enc[1])).astype(jnp.bfloat16)
    return (encoded, (q_heads, k_heads, v_heads, attn_probs, probs_low))


def encode_back(grad_encoded, w_enc, stored):
    q_heads, k_heads, v_heads, attn_probs, probs_low = stored
    item_count, row_length, enc_width = grad_encoded.shape
    head_count = enc_width // ENC_HD
    score_scale = ENC_HD ** (-0.5)
    grad_mixture = project_back(grad_encoded, w_enc[1]).astype(jnp.bfloat16)
    g_heads = grad_mixture.reshape(item_count, row_length, head_count, ENC_HD)
    grad_probs = jnp.einsum("nthd,nshd->nhts", g_heads, v_heads, preferred_element_type=jnp.float32)
    centred = grad_probs - jnp.sum(attn_probs * grad_probs, axis=-1, keepdims=True)
    grad_scores = (attn_probs * centred * score_scale).astype(jnp.bfloat16)
    grad_queries = jnp.einsum(
        "nhts,nshd->nthd", grad_scores, k_heads, preferred_element_type=jnp.float32
    )
    grad_queries = grad_queries.reshape(item_count, row_length, enc_width).astype(jnp.bfloat16)
    grad_keys = jnp.einsum(
        "nhts,nthd->nshd", grad_scores, q_heads, preferred_element_type=jnp.float32
    ).reshape(item_count, -1, enc_width)
    grad_values = jnp.einsum(
        "nhts,nthd->nshd", probs_low, g_heads, preferred_element_type=jnp.float32
    ).reshape(item_count, -1, enc_width)
    grad_rows = grad_encoded.astype(jnp.float32) + project_back(grad_queries, w_enc[0])
    return (grad_rows, jnp.stack([grad_keys, grad_values], axis=2))


def cross_attend(queries, prev_pairs, grad_att):
    stretch_count, stretch_len, inner_part = queries.shape
    head_count = inner_part // HD
    score_scale = HD ** (-0.5)
    q_heads = queries.reshape(stretch_count, stretch_len, head_count, HD)
    k_heads = prev_pairs[0].reshape(stretch_count, -1, head_count, HD)
    v_heads = prev_pairs[1].reshape(stretch_count, -1, head_count, HD)
    g_heads = grad_att.reshape(stretch_count, stretch_len, head_count, HD)
    scores = (
        jnp.einsum("cqhd,ckhd->chqk", q_heads, k_heads, preferred_element_type=jnp.float32)
        * score_scale
    )
    exponent = jnp.exp(scores)
    attn_probs = exponent / jnp.sum(exponent, axis=-1, keepdims=True)
    probs_low = attn_probs.astype(jnp.bfloat16)
    grad_probs = jnp.einsum("cqhd,ckhd->chqk", g_heads, v_heads, preferred_element_type=jnp.float32)
    centred = grad_probs - jnp.sum(attn_probs * grad_probs, axis=-1, keepdims=True)
    grad_scores = (attn_probs * centred * score_scale).astype(jnp.bfloat16)
    grad_q = jnp.einsum("chqk,ckhd->cqhd", grad_scores, k_heads, preferred_element_type=jnp.float32)
    grad_q = grad_q.reshape(stretch_count, stretch_len, inner_part).astype(jnp.bfloat16)
    grad_k = jnp.einsum("chqk,cqhd->ckhd", grad_scores, q_heads, preferred_element_type=jnp.float32)
    grad_v = jnp.einsum("chqk,cqhd->ckhd", probs_low, g_heads, preferred_element_type=jnp.float32)
    grad_pair = jnp.stack(
        [
            grad_k.reshape(stretch_count, -1, inner_part),
            grad_v.reshape(stretch_count, -1, inner_part),
        ]
    )
    return (grad_q, grad_pair.astype(jnp.bfloat16))


def on_device(
    activations, grad_out, database, owners, row_index, w_cond, w_enc, w_query, w_kv, w_out
):
    stretches, pair_count = owners.shape
    token_count, model_width = activations.shape
    stretch_len = token_count // stretches
    db_rows, row_length, enc_width = database.shape
    ret_count = lax.axis_size("ret")
    my_rank = lax.axis_index("ret")
    entries = stretches * pair_count
    capacity = max(2, 5 * entries // (4 * ret_count))
    owner_flat = owners.reshape(-1)
    rows_flat = row_index.reshape(-1)
    positions = jnp.arange(entries, dtype=jnp.int32)
    owner_hot = (owner_flat[:, None] == jnp.arange(ret_count, dtype=jnp.int32)[None, :]).astype(
        jnp.int32
    )
    earlier = jnp.cumsum(owner_hot, axis=0) - owner_hot
    slot_of = jnp.sum(earlier * owner_hot, axis=1)
    global_slot = owner_flat * capacity + slot_of
    slot_ids = jnp.arange(capacity, dtype=jnp.int32)
    matches = ((owner_flat[None, :] == my_rank) & (slot_of[None, :] == slot_ids[:, None])).astype(
        jnp.int32
    )
    filled = jnp.sum(matches, axis=1)
    slot_entry = jnp.sum(matches * positions[None, :], axis=1)
    slot_row = jnp.sum(matches * rows_flat[None, :], axis=1)
    slot_stretch = slot_entry // pair_count
    slot_rows = jnp.take(database, slot_row, axis=0)
    query_full, kv_full, cond_full, out_full = (
        lax.all_gather(w_query, "seq", axis=0, tiled=True),
        lax.all_gather(w_kv, "seq", axis=1, tiled=True),
        lax.all_gather(w_cond, "seq", axis=1, tiled=True),
        lax.all_gather(w_out, "seq", axis=1, tiled=True),
    )
    cond_part = jnp.einsum(
        "td,kde->tke", activations, cond_full, preferred_element_type=jnp.float32
    ).astype(jnp.bfloat16)
    cond_all = lax.all_gather(cond_part, "ret", axis=2, tiled=True)
    cond_stretches = cond_all.reshape(stretches, stretch_len, 2, enc_width)
    cond_mine = jnp.take(cond_stretches, slot_stretch, axis=0)
    encoded_mine, stored = encode_rows(slot_rows, cond_mine, w_enc)
    encoded_all = lax.all_gather(encoded_mine, "ret", axis=0, tiled=True)
    encoded = jnp.take(encoded_all, global_slot, axis=0)
    inner_part = kv_full.shape[2]
    key_value = jnp.einsum(
        "nle,kei->knli", encoded, kv_full, preferred_element_type=jnp.float32
    ).astype(jnp.bfloat16)
    key_value = key_value.reshape(2, stretches, pair_count * row_length, inner_part)
    last_pair = passed_along(key_value[:, stretches - 1], "seq", 1)
    prev_pairs = jnp.concatenate([last_pair[:, None], key_value[:, : stretches - 1]], axis=1)
    queries = (
        project(activations, query_full)
        .astype(jnp.bfloat16)
        .reshape(stretches, stretch_len, inner_part)
    )
    grad_att = (
        project_back(grad_out, out_full)
        .astype(jnp.bfloat16)
        .reshape(stretches, stretch_len, inner_part)
    )
    grad_q, grad_pair = cross_attend(queries, prev_pairs, grad_att)
    back_pair = passed_along(grad_pair[:, 0], "seq", -1)
    own_pair = jnp.concatenate([grad_pair[:, 1:], back_pair[:, None]], axis=1).reshape(
        2, entries, row_length, inner_part
    )
    enc_term = jnp.einsum("knli,kei->nle", own_pair, kv_full, preferred_element_type=jnp.float32)
    row_ids = jnp.arange(db_rows, dtype=jnp.int32)
    stretch_ids = jnp.arange(stretches, dtype=jnp.int32)
    slot_all = jnp.arange(ret_count * capacity, dtype=jnp.int32)
    hits = (global_slot[None, :] == slot_all[:, None]).astype(jnp.int32)
    picked = jnp.sum(hits * positions[None, :], axis=1) + entries * (1 - jnp.sum(hits, axis=1))
    padded = jnp.concatenate([enc_term, jnp.zeros((1, row_length, enc_width), jnp.float32)], axis=0)
    grad_mine = lax.psum_scatter(
        jnp.take(padded, picked, axis=0).astype(jnp.bfloat16),
        "ret",
        scatter_dimension=0,
        tiled=True,
    )
    grad_rows, grad_cond = encode_back(grad_mine, w_enc, stored)
    valid = filled > 0
    row_hot = ((slot_row[None, :] == row_ids[:, None]) & valid[None, :]).astype(jnp.float32)
    stretch_hot = ((slot_stretch[None, :] == stretch_ids[:, None]) & valid[None, :]).astype(
        jnp.float32
    )
    grad_db = jnp.einsum("rm,mle->rle", row_hot, grad_rows, precision=lax.Precision.HIGHEST).astype(
        jnp.bfloat16
    )
    grad_pairs = jnp.einsum(
        "cm,mske->cske", stretch_hot, grad_cond, precision=lax.Precision.HIGHEST
    )
    grad_pairs = grad_pairs.reshape(token_count, 2, enc_width)
    cond_sum = lax.psum_scatter(
        grad_pairs.astype(jnp.bfloat16), "ret", scatter_dimension=2, tiled=True
    )
    grad_q_flat = grad_q.reshape(token_count, inner_part)
    dx_term = project_back(grad_q_flat, query_full)
    dx_term = dx_term + jnp.einsum(
        "tke,kde->td", cond_sum, cond_full, preferred_element_type=jnp.float32
    )
    dx_part = lax.psum_scatter(dx_term.astype(jnp.bfloat16), "ret", scatter_dimension=1, tiled=True)
    token_block = activations
    grad_wq = lax.psum_scatter(
        lax.dot_general(
            token_block, grad_q_flat, (((0,), (0,)), ((), ())), preferred_element_type=jnp.float32
        ).astype(jnp.bfloat16),
        "seq",
        scatter_dimension=0,
        tiled=True,
    )
    token_block = activations
    cond_rows = lax.psum_scatter(
        lax.dot_general(
            token_block, cond_sum, (((0,), (0,)), ((), ())), preferred_element_type=jnp.float32
        ).astype(jnp.bfloat16),
        "seq",
        scatter_dimension=0,
        tiled=True,
    ).astype(jnp.float32)
    grad_wcond = jnp.transpose(cond_rows, (1, 0, 2)).astype(jnp.bfloat16)
    return (dx_part, grad_db, grad_wq, grad_wcond)


def solution(mesh):
    return jax.shard_map(
        on_device,
        mesh=mesh,
        in_specs=(
            P("seq", None),
            P("seq", None),
            P(("seq", "ret"), None, None),
            P("seq", None),
            P("seq", None),
            P(None, "seq", "ret"),
            P(),
            P("seq", "ret"),
            P(None, "seq", "ret"),
            P("ret", "seq"),
        ),
        out_specs=(
            P("seq", "ret"),
            P(("seq", "ret"), None, None),
            P("seq", "ret"),
            P(None, "seq", "ret"),
        ),
        check_vma=False,
    )
```

profile of v0, /device:TPU:0, one launch (start us, length us, event | category | flops | bytes accessed | tf_op | source)
XLA Modules:
  0.0 746.3 jit_solution(9599414340226840424)
XLA Ops:
  8.0 52.9 %all-gather.7.cloned.1.call-done = bf16[2,4096,224]{1,2,0:T(8,128)(2,1)} async-done(((bf16[2,128,224]{1,2,0:T(8,128)(2,1)}), bf16[2,4096,224]{1,2,0:T(8,128)(2,1)}) %all-gather.7.cloned.1.call-update) | async-done | bytes 3670032 | tf_op jit(solution)/shard_map/all_gather | solution.py:142
  60.8 5.4 fusion.140
  70.5 3.0 fusion.49
  74.5 20.9 %all-gather.9.cloned.1.call-done = bf16[512,2,896]{0,2,1:T(8,128)(2,1)} async-done(((bf16[512,2,224]{0,2,1:T(8,128)(2,1)}), bf16[512,2,896]{0,2,1:T(8,128)(2,1)}) %all-gather.9.cloned.1.call-update) | async-done | bytes 1835024 | tf_op jit(solution)/shard_map/all_gather | solution.py:148
  95.4 2.9 copy.120
  98.3 1.4 copy.121
  99.7 2.2 gather_fusion.1
  103.6 1.5 fusion.62
  105.0 3.2 convolution_convert_fusion.5
  108.2 4.7 add_convert_fusion
  115.0 32.0 %all-gather.17.cloned.1.call-done = bf16[512,4096]{1,0:T(8,128)(2,1)} async-done(((bf16[512,128]{1,0:T(8,128)(2,1)}), bf16[512,4096]{1,0:T(8,128)(2,1)}) %all-gather.17.cloned.1.call-update) | async-done | bytes 4194320 | tf_op jit(solution)/shard_map/all_gather | solution.py:143
  147.0 5.8 convolution_convert_fusion.6
  153.7 45.8 %all-gather.11.cloned.1.call-done = bf16[20,128,896]{2,1,0:T(8,128)(2,1)} async-done(((bf16[5,128,896]{2,1,0:T(8,128)(2,1)}), bf16[20,128,896]{2,1,0:T(8,128)(2,1)}) %all-gather.11.cloned.1.call-update) | async-done | bytes 4587536 | tf_op jit(solution)/shard_map/all_gather | solution.py:152
  199.5 5.1 gather_fusion.2
  204.6 41.1 %all-gather.13.cloned.1.call-done = bf16[2,896,512]{2,0,1:T(2,128)(2,1)} async-done(((bf16[2,28,512]{2,0,1:T(2,128)(2,1)}), bf16[2,896,512]{2,0,1:T(2,128)(2,1)}) %all-gather.13.cloned.1.call-update) | async-done | bytes 1835024 | tf_op jit(solution)/shard_map/all_gather | solution.py:141
  245.6 7.2 convert_bitcast_fusion
  252.8 2.4 copy.129
  256.3 2.4 collective-permute-start
  258.7 34.8 %all-gather.15.cloned.1.call-done = bf16[4096,512]{1,0:T(8,128)(2,1)} async-done(((bf16[128,512]{1,0:T(8,128)(2,1)}), bf16[4096,512]{1,0:T(8,128)(2,1)}) %all-gather.15.cloned.1.call-update) | async-done | bytes 4194320 | tf_op jit(solution)/shard_map/all_gather | solution.py:140
  293.5 5.8 convolution_convert_fusion.7
  300.3 2.3 slice.53
  303.4 2.5 pad_maximum_fusion.1
  305.9 2.4 copy.134
  308.3 2.8 copy.131
  311.2 4.3 fusion.96
  316.1 1.3 copy-done.13
  317.5 2.3 convolution_convert_fusion.2
  319.8 16.6 %convolution_convert_fusion.3 = bf16[8,4,128,256]{3,2,1,0:T(8,128)(2,1)} fusion(f32[8,4,64,256]{3,2,1,0:T(8,128)} %fusion.96, bf16[8,64,4,128]{3,2,1,0:T(4,128)(2,1)S(1)} %copy-done.12, f32[8,4,64,256]{3,2,1,0:T(8,128)} %copy-done.13, f32[8,4,64]{2,1,0:T(4,128)S(1)} %get-tuple-element.34), kind=kOutput, calls=%fused_computation.40 | convolution fusion | flops 139987200 | bytes 6823936 | tf_op jit(solution)/shard_map/chqk,cqhd->ckhd/dot_general | solution.py:99
  336.4 2.9 copy.142
  339.2 3.9 copy.141
  344.3 1.3 collective-permute-start.1
  345.7 2.5 collective-permute-done.1
  349.7 4.8 convolution_bitcast_fusion
  354.4 2.4 concatenate.11
  356.9 5.7 gather_fusion.3
  362.5 5.7 select_convert_fusion
  370.6 55.6 %reduce-scatter.9.cloned.1.call-done = bf16[5,128,896]{2,1,0:T(8,128)(2,1)} async-done(((bf16[20,128,896]{2,1,0:T(8,128)(2,1)}), bf16[5,128,896]{2,1,0:T(8,128)(2,1)}) %reduce-scatter.9.cloned.1.call-update) | async-done | bytes 1146896 | tf_op jit(solution)/shard_map/reduce_scatter | solution.py:183
  426.2 4.3 fusion.52
  430.5 1.9 copy.145
  432.4 3.6 convolution_bitcast_fusion.1
  436.0 1.5 fusion.88
  437.4 3.2 convolution_bitcast_fusion.2
  441.9 1.7 copy.178
  443.6 1.4 reshape.283
  445.1 1.5 reshape.282
  446.5 3.6 fusion.28
  450.6 3.7 copy.155
  455.6 53.0 %all-reduce.4.cloned.1.call-done = bf16[512,2,896]{0,1,2:T(2,128)(2,1)} async-done(((bf16[512,2,896]{0,1,2:T(2,128)(2,1)}), bf16[512,2,896]{0,1,2:T(2,128)(2,1)}) %all-reduce.4.cloned.1.call-update) | async-done | bytes 1835024
  508.6 1.3 constant_dynamic-slice_fusion
  509.9 6.1 convolution_convert_fusion.1
  516.1 6.4 copy.185
  524.1 14.8 %fusion.69 = bf16[8,64,4,128]{3,1,2,0:T(8,128)(2,1)S(1)} fusion(bf16[8,256,4,128]{1,3,2,0:T(8,128)(2,1)S(1)} %bitcast.170, f32[8,4,64,256]{3,2,1,0:T(8,128)} %fusion.96, f32[8,4,64,256]{3,2,1,0:T(8,128)} %copy-done.13, f32[8,4,64]{2,1,0:T(4,128)S(1)} %get-tuple-element.34), kind=kOutput, calls=%fused_computation.77 | convolution fusion | flops 139200768 | bytes 6823936 | tf_op jit(solution)/shard_map/chqk,ckhd->cqhd/dot_general | solution.py:97
  539.3 6.7 fusion.3
  546.0 6.5 copy.179
  552.7 4.8 fusion.85
  557.6 4.6 fusion.2
  563.3 3.0 convolution_convert_fusion.4
  566.3 3.0 convert_add_fusion
  569.3 3.1 fusion.31
  572.4 1.5 copy.161
  573.9 30.8 %reduce-scatter.15.cloned.1.call-done = bf16[128,448]{1,0:T(8,128)(2,1)} async-done(((bf16[4096,448]{1,0:T(8,128)(2,1)}), bf16[128,448]{1,0:T(8,128)(2,1)}) %reduce-scatter.15.cloned.1.call-update) | async-done | bytes 114704
  604.7 1.7 copy.186
  606.4 84.2 %reduce-scatter.13.cloned.1.call-done = bf16[128,512]{1,0:T(8,128)(2,1)} async-done(((bf16[4096,512]{1,0:T(8,128)(2,1)}), bf16[128,512]{1,0:T(8,128)(2,1)}) %reduce-scatter.13.cloned.1.call-update) | async-done | bytes 131088
  690.5 49.0 %reduce-scatter.11.cloned.1.call-done = bf16[512,1024]{1,0:T(8,128)(2,1)} async-done(((bf16[512,4096]{1,0:T(8,128)(2,1)}), bf16[512,1024]{1,0:T(8,128)(2,1)}) %reduce-scatter.11.cloned.1.call-update) | async-done | bytes 1048592 | tf_op jit(solution)/shard_map/reduce_scatter | solution.py:210
  (110 shorter events, 24.6 us)
Async XLA Ops:
  7.2 61.6 %copy-start = (bf16[8,128,896]{2,1,0:T(8,128)(2,1)S(1)}, bf16[8,128,896]{2,1,0:T(8,128)(2,1)}, u32[]{:S(2)}) copy-start(bf16[8,128,896]{2,1,0:T(8,128)(2,1)} %param.12) | copy-start | bytes 5505028
  7.2 53.6 %all-gather.7.cloned.1.call-start = ((), (), s32[]{:S(2)}) async-start(), calls=%async_computation.4 | async-start | bytes 3784704 | tf_op jit(solution)/shard_map/all_gather | solution.py:142
  7.9 87.5 %all-gather.9.cloned.1.call-start = ((), (), s32[]{:S(2)}) async-start(), calls=%async_computation.5 | async-start | bytes 2293760 | tf_op jit(solution)/shard_map/all_gather | solution.py:148
  60.8 7.1 copy-start.19
  60.8 7.2 copy-start.18
  67.1 79.8 %all-gather.17.cloned.1.call-start = ((), (), s32[]{:S(2)}) async-start(), calls=%async_computation.9 | async-start | bytes 4325376 | tf_op jit(solution)/shard_map/all_gather | solution.py:143
  67.8 131.6 %all-gather.11.cloned.1.call-start = ((), (), s32[]{:S(2)}) async-start(), calls=%async_computation.6 | async-start | bytes 5734400 | tf_op jit(solution)/shard_map/all_gather | solution.py:152
  69.5 1.0 copy-start.15
  102.9 5.4 copy-start.6
  103.5 4.7 copy-start.8
  113.0 132.7 %all-gather.13.cloned.1.call-start = ((), (), s32[]{:S(2)}) async-start(), calls=%async_computation.7 | async-start | bytes 1892352 | tf_op jit(solution)/shard_map/all_gather | solution.py:141
  113.5 180.0 %all-gather.15.cloned.1.call-start = ((), (), s32[]{:S(2)}) async-start(), calls=%async_computation.8 | async-start | bytes 4325376 | tf_op jit(solution)/shard_map/all_gather | solution.py:140
  114.1 312.0 %reduce-scatter.9.cloned.1.call-start = ((), (), s32[]{:S(2)}) async-start(), calls=%async_computation.10 | async-start | bytes 5734400 | tf_op jit(solution)/shard_map/reduce_scatter | solution.py:183
  256.3 46.2 %collective-permute-start = (bf16[2,256,512]{2,1,0:T(8,128)(2,1)S(1)}, bf16[2,256,512]{2,1,0:T(8,128)(2,1)S(1)}, u32[]{:S(2)}, u32[]{:S(2)}) collective-permute-start(bf16[2,256,512]{2,1,0:T(8,128)(2,1)S(1)} %slice_bitcast_fusion), channel_id=1, source_target_pairs={{0,4},{4,8},{8,12},{12,16},{16,20},{20,24},{24,28},{28,32},{32,36}... | collective-permute-start | bytes 1572872 | tf_op jit(solution)/shard_map/ppermute | solution.py:13
  302.6 0.8 copy-start.17
  311.2 4.3 copy-start.3
  311.2 4.3 copy-start.11
  315.5 2.0 copy-start.10
  316.1 1.3 copy-start.13
  317.5 2.3 copy-start.12
  343.2 5.0 copy-start.2
  344.3 3.8 collective-permute-start.1
  348.1 1.5 copy-start.20
  368.2 1.3 copy-start.14
  368.2 140.4 %all-reduce.4.cloned.1.call-start = ((), (), s32[]{:S(2)}) async-start(), calls=%async_computation.14 | async-start | bytes 3670016
  432.4 3.6 copy-start.9
  440.6 1.3 copy-start.16
  450.5 3.8 copy-start.22
  454.3 150.4 %reduce-scatter.15.cloned.1.call-start = ((), (), s32[]{:S(2)}) async-start(), calls=%async_computation.13 | async-start | bytes 4325376
  522.5 1.6 copy-start.4
  522.5 168.0 %reduce-scatter.13.cloned.1.call-start = ((), (), s32[]{:S(2)}) async-start(), calls=%async_computation.12 | async-start | bytes 4325376
  552.5 187.1 %reduce-scatter.11.cloned.1.call-start = ((), (), s32[]{:S(2)}) async-start(), calls=%async_computation.11 | async-start | bytes 5242880 | tf_op jit(solution)/shard_map/reduce_scatter | solution.py:210
  552.7 4.9 copy-start.5
  562.2 1.1 copy-start.7
  563.3 3.0 copy-start.21
  569.3 170.3 %copy-start.1 = (bf16[8,128,896]{2,1,0:T(8,128)(2,1)S(1)}, bf16[8,128,896]{2,1,0:T(8,128)(2,1)}, u32[]{:S(2)}) copy-start(bf16[8,128,896]{2,1,0:T(8,128)(2,1)} %param.12) | copy-start | bytes 5505028
Sparse Core Ops, SparseCore 0:
  10.2 50.5 all-gather.6
  67.2 28.1 all-gather.8
  97.6 49.3 all-gather.16
  148.5 50.9 all-gather.10
  201.6 43.9 all-gather.12
  247.7 45.7 all-gather.14
  368.4 57.7 reduce-scatter.8
  454.4 54.1 all-reduce.3
  522.6 82.0 reduce-scatter.14
  609.2 81.2 reduce-scatter.12
  693.5 46.0 reduce-scatter.10
where the time goes:
time: 755 us; the launch traced here: 746 us
  waiting for transfers between devices  505 us (67%)
  matrix products  127 us (17%)
  local copies, waits for them, and re-layouts  80.9 us (11%)
  between operations  15.2 us (2%)
  other arithmetic  12.4 us (2%)
    unnamed x14, waiting for transfers between devices  171 us
    reduce_scatter x1, waiting for transfers between devices, on_device(): lax.psum_scatter(jnp.take(padded, picked, axis=0).astype(jnp.bfloat16), '...  55.6 us
    all_gather x1, waiting for transfers between devices, on_device(): lax.all_gather(w_cond, 'seq', axis=1, tiled=True)  52.9 us
    reduce_scatter x1, waiting for transfers between devices, on_device(): lax.psum_scatter(dx_term.astype(jnp.bfloat16), 'ret', scatter_dimension=1...  49 us
    all_gather x1, waiting for transfers between devices, on_device(): encoded_all = lax.all_gather(encoded_mine, 'ret', axis=0, tiled=True)  45.8 us
    all_gather x1, waiting for transfers between devices, on_device(): lax.all_gather(w_kv, 'seq', axis=1, tiled=True)  41.1 us
    all_gather x1, waiting for transfers between devices, on_device(): lax.all_gather(w_query, 'seq', axis=0, tiled=True)  34.8 us
    all_gather x1, waiting for transfers between devices, on_device(): lax.all_gather(w_out, 'seq', axis=1, tiled=True)  32 us
  transfers between devices with their start and end apart: 13, of which 12 were waited for; matrix products, arithmetic and copies ran while one was open for 14% of the time, Pallas kernels for 0%

commit v1 on v0

v1 whole, which is shorter than its diff:
```python
import functools

import jax
import jax.numpy as jnp
from jax import lax
from jax.experimental import pallas as pl
from jax.experimental.pallas import tpu as pltpu
from jax.sharding import PartitionSpec as P

HD = 128
BF = jnp.bfloat16
F32 = jnp.float32
VMEM_LIMIT = 40 * 1024 * 1024


def along_seq(value, steps):
    count = lax.axis_size("seq")
    first, last = (max(0, -steps), min(count, count - steps))
    return lax.ppermute(value, "seq", [(i, i + steps) for i in range(first, last)])


def around_ret(value, steps):
    count = lax.axis_size("ret")
    return lax.ppermute(value, "ret", [(i, (i + steps) % count) for i in range(count)])


def mm(left, right, contract):
    return lax.dot_general(left, right, (contract, ((), ())), preferred_element_type=F32)


NN = ((1,), (0,))
NT = ((1,), (1,))
TN = ((0,), (0,))


def cost(flops, nbytes):
    return pl.CostEstimate(flops=int(flops), bytes_accessed=int(nbytes), transcendentals=0)


def projections_kernel(x_ref, g_ref, w_ref, o_ref, acc_q, acc_g):
    step = pl.program_id(0)
    shards, rows, width = w_ref.shape
    half = width // 2

    @pl.when(step == 0)
    def _():
        acc_q[...] = jnp.zeros_like(acc_q)
        acc_g[...] = jnp.zeros_like(acc_g)

    w = w_ref[...].reshape(shards * rows, width)
    acc_q[...] += mm(x_ref[...], w[:, :half], NN)
    acc_g[...] += mm(g_ref[...], w[:, half:], NN)

    @pl.when(step == pl.num_programs(0) - 1)
    def _():
        o_ref[:, :half] = acc_q[...].astype(BF)
        o_ref[:, half:] = acc_g[...].astype(BF)


def projections(activations, grad_out, gathered, rows):
    tokens, model = activations.shape
    shards, _, width = gathered.shape
    per_step = 4
    depth = per_step * rows
    return pl.pallas_call(
        projections_kernel,
        grid=(shards // per_step,),
        in_specs=[
            pl.BlockSpec((tokens, depth), lambda i: (0, i)),
            pl.BlockSpec((tokens, depth), lambda i: (0, i)),
            pl.BlockSpec((per_step, rows, width), lambda i: (i, 0, 0)),
        ],
        out_specs=pl.BlockSpec((tokens, width), lambda i: (0, 0)),
        out_shape=jax.ShapeDtypeStruct((tokens, width), BF),
        scratch_shapes=[pltpu.VMEM((tokens, width // 2), F32)] * 2,
        compiler_params=pltpu.CompilerParams(vmem_limit_bytes=VMEM_LIMIT),
        cost_estimate=cost(
            2 * tokens * model * width, 2 * (2 * tokens * model + model * width + tokens * width)
        ),
        name="projections",
    )(activations, grad_out, gathered)


def encode_kernel(keep_ref, rows_ref, q_ref, k_ref, v_ref, w_ref, o_ref, mixed):
    enc_width = rows_ref.shape[-1]
    scale = HD ** (-0.5)
    keep = keep_ref[pl.program_id(0)]
    for h in range(enc_width // HD):
        cols = slice(h * HD, (h + 1) * HD)
        scores = mm(q_ref[0, :, cols], k_ref[:, cols], NT) * scale
        exponent = jnp.exp(scores)
        probs = exponent / jnp.sum(exponent, axis=-1, keepdims=True)
        mixed[:, cols] = mm(probs.astype(BF), v_ref[:, cols], NN).astype(BF)
    coded = rows_ref[0].astype(F32) + mm(mixed[...], w_ref[...], NN)
    o_ref[0] = jnp.where(keep > 0, coded, 0.0).astype(BF)


def encode(keep, rows, queries, keys, values, w_back, pair_count):
    entries, length, width = rows.shape
    stretch_len = keys.shape[0] // (entries // pair_count)
    one = pl.BlockSpec((1, length, width), lambda e, keep: (e, 0, 0))
    side = pl.BlockSpec((stretch_len, width), lambda e, keep: (e // pair_count, 0))
    return pl.pallas_call(
        encode_kernel,
        grid_spec=pltpu.PrefetchScalarGridSpec(
            num_scalar_prefetch=1,
            grid=(entries,),
            in_specs=[one, one, side, side, pl.BlockSpec((width, width), lambda e, keep: (0, 0))],
            out_specs=one,
            scratch_shapes=[pltpu.VMEM((length, width), BF)],
        ),
        out_shape=jax.ShapeDtypeStruct(rows.shape, BF),
        compiler_params=pltpu.CompilerParams(vmem_limit_bytes=VMEM_LIMIT),
        cost_estimate=cost(
            2 * entries * length * width * (width + 2 * stretch_len),
            2 * (3 * entries * length * width + width * width),
        ),
        name="encode",
    )(keep, rows, queries, keys, values, w_back)


def encode_back_kernel(
    keep_ref, t0, t1, t2, t3, q_ref, k_ref, v_ref, w_in_ref, w_back_ref,
    rows_out, keys_out, values_out, mixed, enc_q, acc_k, acc_v, *, pair_count,
):
    step = pl.program_id(0)
    enc_width = q_ref.shape[-1]
    scale = HD ** (-0.5)
    keep = keep_ref[step]
    total = (t0[0].astype(F32) + t1[0].astype(F32)) + (t2[0].astype(F32) + t3[0].astype(F32))
    coded = jnp.where(keep > 0, total, 0.0).astype(BF)
    mixed[...] = mm(coded, w_back_ref[...], NT).astype(BF)

    @pl.when(step % pair_count == 0)
    def _():
        acc_k[...] = jnp.zeros_like(acc_k)
        acc_v[...] = jnp.zeros_like(acc_v)

    for h in range(enc_width // HD):
        cols = slice(h * HD, (h + 1) * HD)
        q, k, v, g = q_ref[0, :, cols], k_ref[:, cols], v_ref[:, cols], mixed[:, cols]
        exponent = jnp.exp(mm(q, k, NT) * scale)
        probs = exponent / jnp.sum(exponent, axis=-1, keepdims=True)
        grad_probs = mm(g, v, NT)
        centred = grad_probs - jnp.sum(probs * grad_probs, axis=-1, keepdims=True)
        grad_scores = (probs * centred * scale).astype(BF)
        enc_q[:, cols] = mm(grad_scores, k, NN).astype(BF)
        acc_k[:, cols] += mm(grad_scores, q, TN)
        acc_v[:, cols] += mm(probs.astype(BF), g, TN)
    rows_out[0] = (coded.astype(F32) + mm(enc_q[...], w_in_ref[...], NT)).astype(BF)

    @pl.when(step % pair_count == pair_count - 1)
    def _():
        keys_out[...] = acc_k[...].astype(BF)
        values_out[...] = acc_v[...].astype(BF)


def encode_back(keep, terms, queries, keys, values, w_in, w_back, pair_count):
    entries, length, width = queries.shape
    stretch_len = keys.shape[0] // (entries // pair_count)
    one = pl.BlockSpec((1, length, width), lambda e, keep: (e, 0, 0))
    side = pl.BlockSpec((stretch_len, width), lambda e, keep: (e // pair_count, 0))
    whole = pl.BlockSpec((width, width), lambda e, keep: (0, 0))
    return pl.pallas_call(
        functools.partial(encode_back_kernel, pair_count=pair_count),
        grid_spec=pltpu.PrefetchScalarGridSpec(
            num_scalar_prefetch=1,
            grid=(entries,),
            in_specs=[one] * 5 + [side, side, whole, whole],
            out_specs=[one, side, side],
            scratch_shapes=[pltpu.VMEM((length, width), BF)] * 2
            + [pltpu.VMEM((stretch_len, width), F32)] * 2,
        ),
        out_shape=[
            jax.ShapeDtypeStruct(queries.shape, BF),
            jax.ShapeDtypeStruct(keys.shape, BF),
            jax.ShapeDtypeStruct(keys.shape, BF),
        ],
        compiler_params=pltpu.CompilerParams(vmem_limit_bytes=VMEM_LIMIT),
        cost_estimate=cost(
            4 * entries * length * width * (width + 3 * stretch_len),
            2 * (6 * entries * length * width + 2 * width * width),
        ),
        name="encode_back",
    )(keep, *terms, queries, keys, values, w_in, w_back)


def attend_kernel(place_ref, coded_ref, w_ref, qg_ref, *refs):
    term_out, grad_q_out, kv, grad_kv = refs[-4:]
    inner = qg_ref.shape[1] // 2
    scale = HD ** (-0.5)
    span = coded_ref.shape[0] * coded_ref.shape[1]
    coded = coded_ref[...].reshape(span, coded_ref.shape[2])
    kv[...] = mm(coded, w_ref[...], NN).astype(BF)
    for h in range(inner // HD):
        cols = slice(h * HD, (h + 1) * HD)
        right = slice(inner + h * HD, inner + (h + 1) * HD)
        q, g, k, v = qg_ref[:, cols], qg_ref[:, right], kv[:, cols], kv[:, right]
        exponent = jnp.exp(mm(q, k, NT) * scale)
        probs = exponent / jnp.sum(exponent, axis=-1, keepdims=True)
        grad_probs = mm(g, v, NT)
        centred = grad_probs - jnp.sum(probs * grad_probs, axis=-1, keepdims=True)
        grad_scores = (probs * centred * scale).astype(BF)
        grad_q_out[:, cols] = mm(grad_scores, k, NN).astype(BF)
        grad_kv[:, cols] = mm(grad_scores, q, TN).astype(BF)
        grad_kv[:, right] = mm(probs.astype(BF), g, TN).astype(BF)
    term = mm(grad_kv[...], w_ref[...], NT).astype(BF)
    term_out[...] = term.reshape(term_out.shape)


def attend(place, coded, w_kv, queries_grads, grad_q, pair_count):
    entries, length, width = coded.shape
    tokens, both = queries_grads.shape
    inner = both // 2
    stretches = entries // pair_count
    stretch_len = tokens // (4 * stretches)
    span = pair_count * length
    coded_spec = pl.BlockSpec((pair_count, length, width), lambda t, place: (t, 0, 0))
    at_place = lambda t, place: (place[0] * stretches + t, 0)
    in_specs = [
        coded_spec,
        pl.BlockSpec((width, both), lambda t, place: (0, 0)),
        pl.BlockSpec((stretch_len, both), at_place),
    ]
    operands = [coded, w_kv, queries_grads]
    aliases = {}
    if grad_q is not None:
        in_specs.append(pl.BlockSpec(memory_space=pl.ANY))
        operands.append(grad_q)
        aliases = {4: 1}
    return pl.pallas_call(
        attend_kernel,
        grid_spec=pltpu.PrefetchScalarGridSpec(
            num_scalar_prefetch=1,
            grid=(stretches,),
            in_specs=in_specs,
            out_specs=[coded_spec, pl.BlockSpec((stretch_len, inner), at_place)],
            scratch_shapes=[pltpu.VMEM((span, both), BF)] * 2,
        ),
        out_shape=[
            jax.ShapeDtypeStruct(coded.shape, BF),
            jax.ShapeDtypeStruct((tokens, inner), BF),
        ],
        input_output_aliases=aliases,
        compiler_params=pltpu.CompilerParams(vmem_limit_bytes=VMEM_LIMIT),
        cost_estimate=cost(
            4 * entries * length * width * both + 10 * stretches * stretch_len * span * inner,
            2 * (2 * entries * length * width + width * both + 3 * tokens * inner // 4),
        ),
        name="attend",
    )(place, *operands)


def grad_x_kernel(place_ref, q_ref, c_ref, w_ref, wc_ref, o_ref):
    shards, rows, width = w_ref.shape
    w = w_ref[...].reshape(shards * rows, width)
    o_ref[...] = (mm(q_ref[...], w, NT) + mm(c_ref[...], wc_ref[...], NT)).astype(BF)


def grad_x_block(place, grad_q, cond_sum, gathered, cond_full, rows, blocks):
    tokens, inner = grad_q.shape
    model, cond_width = cond_full.shape
    columns = model // blocks
    tiles = 2
    tile = columns // tiles
    return pl.pallas_call(
        grad_x_kernel,
        grid_spec=pltpu.PrefetchScalarGridSpec(
            num_scalar_prefetch=1,
            grid=(tiles,),
            in_specs=[
                pl.BlockSpec((tokens, inner), lambda i, place: (0, 0)),
                pl.BlockSpec((tokens, cond_width), lambda i, place: (0, 0)),
                pl.BlockSpec(
                    (tile // rows, rows, inner), lambda i, place: (place[0] * tiles + i, 0, 0)
                ),
                pl.BlockSpec((tile, cond_width), lambda i, place: (place[0] * tiles + i, 0)),
            ],
            out_specs=pl.BlockSpec((tokens, tile), lambda i, place: (0, i)),
        ),
        out_shape=jax.ShapeDtypeStruct((tokens, columns), BF),
        compiler_params=pltpu.CompilerParams(vmem_limit_bytes=VMEM_LIMIT),
        cost_estimate=cost(
            2 * tokens * columns * (inner + cond_width),
            2 * (tokens * (inner + cond_width + columns) + columns * (inner + cond_width)),
        ),
        name="grad_x_block",
    )(place, grad_q, cond_sum, gathered, cond_full)


def on_device(
    activations, grad_out, database, owners, row_index, w_cond, w_enc, w_query, w_kv, w_out
):
    stretches, pair_count = owners.shape
    tokens, model = activations.shape
    stretch_len = tokens // stretches
    db_rows, length, enc_width = database.shape
    ranks = lax.axis_size("ret")
    rank = lax.axis_index("ret")
    block = lax.axis_index("seq")
    home = stretches // ranks
    shard_rows, inner = w_query.shape
    cond_width = 2 * w_cond.shape[2]
    kv_rows = w_kv.shape[1]
    kv_pad = -kv_rows % 16

    cond_shard = jnp.transpose(w_cond, (1, 0, 2)).reshape(shard_rows, cond_width)
    cond_full = lax.all_gather(cond_shard, "seq", axis=0, tiled=True)
    kv_shard = jnp.pad(
        jnp.transpose(w_kv, (1, 0, 2)).reshape(kv_rows, 2 * inner), ((0, kv_pad), (0, 0))
    )
    packed = jnp.concatenate(
        [jnp.concatenate([w_query, w_out.T], axis=1), kv_shard], axis=0
    )
    gathered = lax.all_gather(packed, "seq", axis=0, tiled=False)
    kv_full = gathered[:, shard_rows : shard_rows + kv_rows].reshape(-1, 2 * inner)

    naming = jnp.stack([owners, row_index])
    naming = jnp.concatenate([along_seq(naming[:, -1:], 1), naming[:, :-1]], axis=1)
    owners_prev, rows_prev = naming[0], naming[1]
    tokens_prev = jnp.concatenate(
        [along_seq(activations[tokens - stretch_len :], 1), activations[: tokens - stretch_len]],
        axis=0,
    )
    last_row = jnp.sum(jnp.where(owners[-1] == rank, row_index[-1], 0))
    row_before = along_seq(lax.dynamic_slice_in_dim(database, last_row, 1, axis=0), 1)
    table = jnp.concatenate([database, row_before], axis=0)
    wanted = jnp.sum(jnp.where(owners_prev == rank, rows_prev, 0), axis=1)
    wanted = jnp.where(jnp.arange(stretches) == 0, db_rows, wanted)

    def rows_for(target):
        places = lax.dynamic_slice_in_dim(wanted, target * home, home)
        return jnp.take(table, places, axis=0)

    by_distance = [rows_for(rank)] + [
        around_ret(rows_for((rank + d) % ranks), d) for d in range(1, ranks)
    ]
    owners_home = lax.dynamic_slice_in_dim(owners_prev, rank * home, home)
    distance = (rank - owners_home) % ranks
    pick = (distance * home + jnp.arange(home)[:, None]).reshape(-1)
    rows_home = jnp.take(
        jnp.stack(by_distance).reshape(ranks * home, length, enc_width), pick, axis=0
    )
    entries = home * pair_count
    enc_queries = (
        mm(rows_home.reshape(entries * length, enc_width), w_enc[0], NN)
        .astype(BF)
        .reshape(rows_home.shape)
    )
    real = (block > 0) | (rank > 0) | (jnp.arange(entries) >= pair_count)
    keep = real.astype(jnp.int32)

    cond_part = mm(tokens_prev, cond_full, NN).astype(BF)
    home_tokens = home * stretch_len
    cond_home = lax.all_to_all(
        cond_part.reshape(ranks, home_tokens, cond_width), "ret", split_axis=0, concat_axis=0
    ).reshape(ranks, home_tokens, 2, cond_width // 2)
    cond_home = jnp.transpose(cond_home, (2, 1, 0, 3)).reshape(2, home_tokens, enc_width)
    cond_keys, cond_values = cond_home[0], cond_home[1]
    coded = encode(keep, rows_home, enc_queries, cond_keys, cond_values, w_enc[1], pair_count)

    queries_grads = projections(activations, grad_out, gathered, shard_rows)

    order = [0, 1, ranks - 1, 2]
    arrived = {d: (around_ret(coded, d) if d else coded) for d in order}
    grad_q, terms = None, {}
    for d in order:
        place = jnp.reshape((rank - d) % ranks, (1,)).astype(jnp.int32)
        term, grad_q = attend(place, arrived[d], kv_full, queries_grads, grad_q, pair_count)
        terms[d] = around_ret(term, -d) if d else term

    grad_wq = lax.psum_scatter(
        mm(activations, grad_q, TN).astype(BF), "seq", scatter_dimension=0, tiled=True
    )

    grad_rows, grad_keys, grad_values = encode_back(
        keep, [terms[d] for d in order], enc_queries, cond_keys, cond_values,
        w_enc[0], w_enc[1], pair_count,
    )

    cond_grad = jnp.stack([grad_keys, grad_values]).reshape(
        2, home_tokens, ranks, cond_width // 2
    )
    cond_grad = jnp.transpose(cond_grad, (2, 1, 0, 3)).reshape(ranks, home_tokens, cond_width)
    cond_sum = lax.all_to_all(cond_grad, "ret", split_axis=0, concat_axis=0).reshape(
        tokens, cond_width
    )
    cond_rows = lax.psum_scatter(
        mm(tokens_prev, cond_sum, TN).astype(BF), "seq", scatter_dimension=0, tiled=True
    )
    grad_wcond = jnp.transpose(cond_rows.reshape(shard_rows, 2, cond_width // 2), (1, 0, 2))
    cond_own = jnp.concatenate(
        [cond_sum[stretch_len:], along_seq(cond_sum[:stretch_len], -1)], axis=0
    )

    grad_rows = grad_rows.reshape(home, pair_count, length, enc_width)

    def rows_to(target):
        hits = (owners_home == target)[:, :, None, None]
        return jnp.sum(jnp.where(hits, grad_rows, jnp.zeros((), BF)).astype(F32), axis=1).astype(BF)

    returned = [rows_to(rank)] + [
        around_ret(rows_to((rank + d) % ranks), d) for d in range(1, ranks)
    ]

    def share(d):
        place = jnp.reshape((rank + d) % ranks, (1,)).astype(jnp.int32)
        return grad_x_block(place, grad_q, cond_own, gathered, cond_full, shard_rows, ranks)

    shares = [around_ret(share(d), d) for d in (2, 1, ranks - 1)] + [share(0)]
    grad_x = sum(part.astype(F32) for part in shares).astype(BF)

    returned = jnp.stack(returned)
    back_order = (rank - jnp.arange(ranks)) % ranks
    returned = jnp.take(returned, back_order, axis=0).reshape(stretches, length, enc_width)
    row_after = along_seq(returned[:1], -1)
    returned = jnp.concatenate([returned[1:], row_after], axis=0)
    mine = jnp.sum(jnp.where(owners == rank, row_index, 0), axis=1)
    named = jnp.any(owners == rank, axis=1)
    hits = (jnp.arange(db_rows)[:, None] == mine[None, :]) & named[None, :]
    grad_db = jnp.einsum(
        "rm,mle->rle", hits.astype(BF), returned, preferred_element_type=F32
    ).astype(BF)
    return (grad_x, grad_db, grad_wq, grad_wcond)


def solution(mesh):
    return jax.shard_map(
        on_device,
        mesh=mesh,
        in_specs=(
            P("seq", None),
            P("seq", None),
            P(("seq", "ret"), None, None),
            P("seq", None),
            P("seq", None),
            P(None, "seq", "ret"),
            P(),
            P("seq", "ret"),
            P(None, "seq", "ret"),
            P("ret", "seq"),
        ),
        out_specs=(
            P("seq", "ret"),
            P(("seq", "ret"), None, None),
            P("seq", "ret"),
            P(None, "seq", "ret"),
        ),
        check_vma=False,
    )
```

time: 755 us -> 441 us (0.58)
  waiting for transfers between devices: 505 us -> 183 us
  matrix products: 127 us -> 22 us
  Pallas kernels: 0 us -> 70.4 us
  starting transfers between devices: 5.42 us -> 37.4 us
  blocking collectives: 0 us -> 12.9 us
  local copies, waits for them, and re-layouts: 80.9 us -> 70.5 us
  other arithmetic: 12.4 us -> 20.3 us
    all_gather x6 -> x2, waiting for transfers between devices: 227 us -> 17 us  [the longest x1 17 us: on_device(): gathered = lax.all_gather(packed, 'seq', axis=0, tiled=False)]
    reduce_scatter x2 -> x0, waiting for transfers between devices: 105 us -> none  [the longest x1 55.6 us: on_device(): lax.psum_scatter(jnp.take(padded, picked, axis=0).astype(jnp.bfloat16), '...]
    dot_general x25 -> x5, matrix products: 122 us -> 22 us  [the longest x4 21 us: mm(): lax.dot_general(left, right, (contract, ((), ())), preferred_element_type...]
    unnamed x14 -> x6, waiting for transfers between devices: 171 us -> 77.5 us
    ppermute x2 -> x20, waiting for transfers between devices: 2.46 us -> 83.3 us  [the longest x15 81.7 us: around_ret(): lax.ppermute(value, 'ret', [(i, (i + steps) % count) for i in range(count)])]
    pallas_call x0 -> x11, Pallas kernels: none -> 70.4 us  [the longest x4 27.7 us: attend(): pl.pallas_call(attend_kernel, grid_spec=pltpu.PrefetchScalarGridSpec(num_...]
    ppermute x2 -> x20, starting transfers between devices: 3.66 us -> 32.8 us  [the longest x15 22 us: around_ret(): lax.ppermute(value, 'ret', [(i, (i + steps) % count) for i in range(count)])]
    another operation x10 -> x0, local copies, waits for them, and re-layouts: 15.3 us -> none  [the longest x2 6.81 us: cross_attend(): jnp.stack([grad_k.reshape(stretch_count, -1, inner_part), grad_v.reshape(...]
  transfers between devices with their start and end apart: 13 -> 25, of which waited for: 12 -> 13; matrix products, arithmetic and copies ran while one was open for 14% -> 19% of each run, Pallas kernels for 0% -> 11%
where the time goes in v1:
time: 441 us; the launch traced here: 433 us
  waiting for transfers between devices  183 us (41%)
  local copies, waits for them, and re-layouts  70.5 us (16%)
  Pallas kernels  70.4 us (16%)
  starting transfers between devices  37.4 us (8%)
  matrix products  22 us (5%)
  other arithmetic  20.3 us (5%)
  between operations  16.6 us (4%)
  blocking collectives  12.9 us (3%)
    ppermute x15, waiting for transfers between devices, around_ret(): lax.ppermute(value, 'ret', [(i, (i + steps) % count) for i in range(count)])  81.7 us
    unnamed x6, waiting for transfers between devices  77.5 us
    unnamed x46, local copies, waits for them, and re-layouts  32.2 us
    pallas_call x4, Pallas kernels, attend(): pl.pallas_call(attend_kernel, grid_spec=pltpu.PrefetchScalarGridSpec(num_...  27.7 us
    ppermute x15, starting transfers between devices, around_ret(): lax.ppermute(value, 'ret', [(i, (i + steps) % count) for i in range(count)])  22 us
    dot_general x4, matrix products, mm(): lax.dot_general(left, right, (contract, ((), ())), preferred_element_type...  21 us
    all_gather x1, waiting for transfers between devices, on_device(): gathered = lax.all_gather(packed, 'seq', axis=0, tiled=False)  17 us
    pallas_call x1, Pallas kernels, encode_back(): pl.pallas_call(functools.partial(encode_back_kernel, pair_count=pair_coun...  15.9 us
  transfers between devices with their start and end apart: 25, of which 13 were waited for; matrix products, arithmetic and copies ran while one was open for 19% of the time, Pallas kernels for 11%

profile of v1, /device:TPU:0, one launch (start us, length us, event | category | flops | bytes accessed | tf_op | source)
XLA Modules:
  0.0 432.9 jit_solution(7192674929236028956)
XLA Ops:
  7.2 1.8 copy.54
  11.0 1.7 fusion.12
  14.8 1.4 fusion.18
  18.2 4.2 collective-permute-start.1
  22.4 1.9 slice.62
  24.3 2.7 collective-permute-start.5
  27.0 4.3 slice.63
  31.5 1.4 constant_dynamic-update-slice_fusion.1
  32.9 3.4 slice_bitcast_fusion.1
  37.6 2.2 gather_fusion.3
  40.7 1.6 collective-permute-start.2
  42.3 2.2 gather_fusion.4
  45.4 2.9 collective-permute-start.3
  48.3 2.2 gather_fusion.5
  52.8 2.2 gather_fusion.2
  55.5 11.0 %collective-permute-done.3 = bf16[2,128,896]{2,1,0:T(8,128)(2,1)S(1)} collective-permute-done((bf16[2,128,896]{2,1,0:T(8,128)(2,1)}, bf16[2,128,896]{2,1,0:T(8,128)(2,1)S(1)}, u32[]{:S(2)}, u32[]{:S(2)}) %collective-permute-start.3) | collective-permute-done | bytes 458784 | tf_op jit(solution)/shard_map/ppermute | solution.py:24
  66.5 2.5 collective-permute-done.4
  69.8 1.6 pad_maximum_fusion.3
  71.4 1.6 gather_fusion
  72.9 5.6 %fusion.10 = bf16[56,4,8,128]{3,2,1,0:T(8,128)(2,1)S(1)} fusion(bf16[4096,448]{1,0:T(8,128)(2,1)} %all-gather.4.cloned.1.call-done.wc_ref, bf16[448,4096]{1,0:T(8,128)(2,1)} %slice.63, bf16[64,4096]{1,0:T(8,128)(2,1)} %collective-permute-done.5), kind=kOutput, calls=%fused_computation.24 | convolution fusion | flops 1887666176 | bytes 8323072 | tf_op jit(solution)/shard_map/dot_general | solution.py:28
  79.4 4.4 %all-to-all-start = ((bf16[4,128,448]{1,2,0:T(8,128)(2,1)}), bf16[4,128,448]{1,2,0:T(8,128)(2,1)S(1)}, u32[]{:S(2)}, u32[]{:S(2)}) async-start(bf16[4,128,448]{1,2,0:T(8,128)(2,1)} %bitcast.79), calls=%async_computation | async-start | bytes 917504 | tf_op jit(solution)/shard_map/all_to_all | solution.py:355
  84.0 2.6 convolution_convert_fusion.2
  87.5 5.1 %all-to-all-done = bf16[4,128,448]{1,2,0:T(8,128)(2,1)S(1)} async-done(((bf16[4,128,448]{1,2,0:T(8,128)(2,1)}), bf16[4,128,448]{1,2,0:T(8,128)(2,1)S(1)}, u32[]{:S(2)}, u32[]{:S(2)}) %all-to-all-start) | async-done | bytes 458784 | tf_op jit(solution)/shard_map/all_to_all | solution.py:355
  93.0 1.4 copy-done.6
  94.3 5.3 %encode.1.coded_ref = bf16[4,128,896]{2,1,0:T(8,128)(2,1)} custom-call(s32[4]{0:T(128)S(1)} %or_convert_fusion.keep_ref, bf16[4,128,896]{2,1,0:T(8,128)(2,1)S(1)} %copy-done.6, bf16[4,128,896]{2,1,0:T(8,128)(2,1)S(1)} %bitcast.80, bf16[128,896]{1,0:T(8,128)(2,1)S(1)} %copy.56.k_ref, bf16[128,896]{1,0:T(8,128)(2,1)S(1)} %copy.57.v_ref, ...), custom_call_target="tpu_custom_call" | custom-call | flops 939524096 | bytes 4358144 | tf_op jit(solution)/shard_map/encode/pallas_call | solution.py:103
  100.1 2.9 collective-permute-start.7
  103.1 17.0 %all-gather.6.cloned.1.call-done = bf16[5120,1024]{1,0:T(8,128)(2,1)} async-done(((bf16[160,1024]{1,0:T(8,128)(2,1)}), bf16[5120,1024]{1,0:T(8,128)(2,1)}) %all-gather.6.cloned.1.call-update) | async-done | bytes 10485776 | tf_op jit(solution)/shard_map/all_gather | solution.py:315
  120.1 3.2 slice.90
  123.3 3.7 reshape.295.w_ref
  127.0 2.2 copy-done.2
  129.2 2.2 copy-done.4
  131.4 9.5 %projections.1.qg_ref = bf16[512,1024]{1,0:T(8,128)(2,1)S(1)} custom-call(bf16[512,4096]{1,0:T(8,128)(2,1)S(1)} %copy-done.2, bf16[512,4096]{1,0:T(8,128)(2,1)S(1)} %copy-done.4, bf16[32,160,1024]{2,1,0:T(8,128)(2,1)} %bitcast.84), custom_call_target="tpu_custom_call" | custom-call | flops 4294967296 | bytes 17825792 | tf_op jit(solution)/shard_map/projections/pallas_call | solution.py:65
  140.9 6.9 %attend.4 = (bf16[4,128,896]{2,1,0:T(8,128)(2,1)S(1)}, bf16[512,512]{1,0:T(8,128)(2,1)S(1)}) custom-call(s32[1]{0:T(128)} %bitcast.26.place_ref, bf16[4,128,896]{2,1,0:T(8,128)(2,1)} %encode.1.coded_ref, bf16[896,1024]{1,0:T(8,128)(2,1)S(1)} %copy-done.7, bf16[512,1024]{1,0:T(8,128)(2,1)S(1)} %projections.1.qg_ref), custom_call_target="tpu_custom_call" | custom-call | flops 2046820352 | bytes 4063232 | tf_op jit(solution)/shard_map/attend/pallas_call | solution.py:231
  147.8 6.9 %attend.5 = (bf16[4,128,896]{2,1,0:T(8,128)(2,1)S(1)}, bf16[512,512]{1,0:T(8,128)(2,1)S(1)}) custom-call(s32[1]{0:T(128)} %bitcast.25.place_ref, bf16[4,128,896]{2,1,0:T(8,128)(2,1)} %collective-permute-done.8.coded_ref, bf16[896,1024]{1,0:T(8,128)(2,1)S(1)} %copy-done.7, bf16[512,1024]{1,0:T(8,128)(2,1)S(1)} %projections.1.qg_ref, ...), custom_call_target="tpu_custom_call", output_to_operand_aliasing={{1}: (4, {})} | custom-call | flops 2046820352 | bytes 4063232 | tf_op jit(solution)/shard_map/attend/pallas_call | solution.py:231
  154.7 6.9 %attend.6 = (bf16[4,128,896]{2,1,0:T(8,128)(2,1)S(1)}, bf16[512,512]{1,0:T(8,128)(2,1)S(1)}) custom-call(s32[1]{0:T(128)} %bitcast.24.place_ref, bf16[4,128,896]{2,1,0:T(8,128)(2,1)} %collective-permute-done.7.coded_ref, bf16[896,1024]{1,0:T(8,128)(2,1)S(1)} %copy-done.7, bf16[512,1024]{1,0:T(8,128)(2,1)S(1)} %projections.1.qg_ref, ...), custom_call_target="tpu_custom_call", output_to_operand_aliasing={{1}: (4, {})} | custom-call | flops 2046820352 | bytes 4063232 | tf_op jit(solution)/shard_map/attend/pallas_call | solution.py:231
  161.6 7.0 %attend.7 = (bf16[4,128,896]{2,1,0:T(8,128)(2,1)S(1)}, bf16[512,512]{1,0:T(8,128)(2,1)S(1)}) custom-call(s32[1]{0:T(128)} %bitcast.1.place_ref, bf16[4,128,896]{2,1,0:T(8,128)(2,1)} %collective-permute-done.6.coded_ref, bf16[896,1024]{1,0:T(8,128)(2,1)S(1)} %copy-done.7, bf16[512,1024]{1,0:T(8,128)(2,1)S(1)} %projections.1.qg_ref, ...), custom_call_target="tpu_custom_call", output_to_operand_aliasing={{1}: (4, {})} | custom-call | flops 2046820352 | bytes 4063232 | tf_op jit(solution)/shard_map/attend/pallas_call | solution.py:231
  168.6 3.1 collective-permute-start.11
  172.3 2.7 collective-permute-start.9
  175.0 18.5 %collective-permute-done.11.t3 = bf16[4,128,896]{2,1,0:T(8,128)(2,1)S(1)} collective-permute-done((bf16[4,128,896]{2,1,0:T(8,128)(2,1)S(1)}, bf16[4,128,896]{2,1,0:T(8,128)(2,1)S(1)}, u32[]{:S(2)}, u32[]{:S(2)}) %collective-permute-start.11) | collective-permute-done | bytes 917536 | tf_op jit(solution)/shard_map/ppermute | solution.py:24
  193.4 19.0 %collective-permute-done.10.t2 = bf16[4,128,896]{2,1,0:T(8,128)(2,1)S(1)} collective-permute-done((bf16[4,128,896]{2,1,0:T(8,128)(2,1)S(1)}, bf16[4,128,896]{2,1,0:T(8,128)(2,1)S(1)}, u32[]{:S(2)}, u32[]{:S(2)}) %collective-permute-start.10) | collective-permute-done | bytes 917536 | tf_op jit(solution)/shard_map/ppermute | solution.py:24
  212.5 15.9 %encode_back.1 = (bf16[4,128,896]{2,1,0:T(8,128)(2,1)S(1)}, bf16[128,896]{1,0:T(8,128)(2,1)S(1)}, bf16[128,896]{1,0:T(8,128)(2,1)S(1)}) custom-call(s32[4]{0:T(128)S(1)} %or_convert_fusion.keep_ref, bf16[4,128,896]{2,1,0:T(8,128)(2,1)S(1)} %get-tuple-element.20.t0, bf16[4,128,896]{2,1,0:T(8,128)(2,1)S(1)} %collective-permute-done.9.t1, ...), custom_call_target="tpu_custom_call" | custom-call | flops 1996488704 | bytes 8716288 | tf_op jit(solution)/shard_map/encode_back/pallas_call | solution.py:164
  233.0 12.9 %all_to_all.10 = bf16[4,128,448]{1,2,0:T(8,128)(2,1)S(1)} all-to-all(bf16[4,128,448]{1,2,0:T(8,128)(2,1)S(1)} %bitcast.96), channel_id=1, replica_groups=mesh['seq'=32,'ret'=4] {'ret'}, dimensions={0} | all-to-all | bytes 917504 | tf_op jit(solution)/shard_map/all_to_all | solution.py:385
  246.1 6.1 %convolution_convert_fusion.1 = bf16[4096,448]{0,1:T(8,128)(2,1)} fusion(bf16[512,448]{1,0:T(8,128)(2,1)S(1)} %bitcast.91, bf16[448,4096]{1,0:T(8,128)(2,1)} %slice.63, bf16[64,4096]{1,0:T(8,128)(2,1)} %collective-permute-done.5), kind=kOutput, calls=%fused_computation.7 | convolution fusion | flops 1889271808 | bytes 8323072 | tf_op jit(solution)/shard_map/dot_general | solution.py:28
  252.2 6.4 %copy.75 = bf16[4096,448]{1,0:T(8,128)(2,1)} copy(bf16[4096,448]{0,1:T(8,128)(2,1)} %convolution_convert_fusion.1) | data formatting | bytes 7340032
  258.7 6.7 %fusion = bf16[4096,512]{0,1:T(8,128)(2,1)} fusion(bf16[512,512]{1,0:T(8,128)(2,1)S(1)} %get-tuple-element.19.q_ref, bf16[512,4096]{1,0:T(8,128)(2,1)} %x_ref.1), kind=kOutput, calls=%fused_computation.8 | convolution fusion | flops 2149580800 | bytes 8912896 | tf_op jit(solution)/shard_map/dot_general | solution.py:28
  265.4 6.6 %copy.73 = bf16[4096,512]{1,0:T(8,128)(2,1)} copy(bf16[4096,512]{0,1:T(8,128)(2,1)} %fusion) | data formatting | bytes 8388608
  273.1 2.0 select_reduce_fusion.3
  275.7 2.1 collective-permute-start.17
  280.2 1.6 collective-permute-done.12
  281.9 2.3 copy-done
  284.2 2.6 grad_x_block.4
  286.9 2.6 collective-permute-start.13
  289.5 3.4 grad_x_block.5
  292.9 3.4 grad_x_block.6
  296.2 23.2 %collective-permute-done.16 = bf16[2,128,896]{2,1,0:T(8,128)(2,1)} collective-permute-done((bf16[2,128,896]{2,1,0:T(8,128)(2,1)}, bf16[2,128,896]{2,1,0:T(8,128)(2,1)}, u32[]{:S(2)}, u32[]{:S(2)}) %collective-permute-start.16) | collective-permute-done | bytes 458784 | tf_op jit(solution)/shard_map/ppermute | solution.py:24
  319.7 2.8 pad_maximum_fusion.4
  322.5 3.5 gather_fusion.1
  326.0 2.8 copy_select_fusion
  330.5 2.6 grad_x_block.7
  334.6 1.5 copy.70
  336.1 6.6 %collective-permute-done.14 = bf16[512,1024]{1,0:T(8,128)(2,1)} collective-permute-done((bf16[512,1024]{1,0:T(8,128)(2,1)}, bf16[512,1024]{1,0:T(8,128)(2,1)}, u32[]{:S(2)}, u32[]{:S(2)}) %collective-permute-start.14) | collective-permute-done | bytes 1048608 | tf_op jit(solution)/shard_map/ppermute | solution.py:24
  343.1 3.7 add_convert_fusion
  346.9 1.7 copy.76
  348.5 77.4 %reduce-scatter.7.cloned.1.call-done = bf16[128,512]{1,0:T(8,128)(2,1)} async-done(((bf16[4096,512]{1,0:T(8,128)(2,1)}), bf16[128,512]{1,0:T(8,128)(2,1)}) %reduce-scatter.7.cloned.1.call-update) | async-done | bytes 131088
  (124 shorter events, 27.1 us)
Async XLA Ops:
  7.2 11.0 %copy-start.13 = (bf16[8,128,896]{2,1,0:T(8,128)(2,1)S(1)}, bf16[8,128,896]{2,1,0:T(8,128)(2,1)}, u32[]{:S(2)}) copy-start(bf16[8,128,896]{2,1,0:T(8,128)(2,1)} %param.14) | copy-start | bytes 5505028
  7.2 65.8 %all-gather.4.cloned.1.call-start = ((), (), s32[]{:S(2)}) async-start(), calls=%async_computation.4 | async-start | bytes 4325376 | tf_op jit(solution)/shard_map/all_gather | solution.py:308
  9.0 111.1 %all-gather.6.cloned.1.call-start = ((), (), s32[]{:S(2)}) async-start(), calls=%async_computation.5 | async-start | bytes 10813440 | tf_op jit(solution)/shard_map/all_gather | solution.py:315
  13.5 22.8 %collective-permute-start = (s32[2,1,2]{1,2,0:T(2,128)S(1)}, s32[2,1,2]{1,2,0:T(2,128)S(1)}, u32[]{:S(2)}, u32[]{:S(2)}) collective-permute-start(s32[2,1,2]{1,2,0:T(2,128)S(1)} %slice_add_fusion), channel_id=1, source_target_pairs={{0,4},{4,8},{8,12},{12,16},{16,20},{20,24},{24,28},{28,32},{32,36}... | collective-permute-start | bytes 56 | tf_op jit(solution)/shard_map/ppermute | solution.py:19
  18.2 18.7 %collective-permute-start.1 = (bf16[1,128,896]{2,1,0:T(8,128)(2,1)S(1)}, bf16[1,128,896]{2,1,0:T(8,128)(2,1)S(1)}, u32[]{:S(2)}, u32[]{:S(2)}) collective-permute-start(bf16[1,128,896]{2,1,0:T(8,128)(2,1)S(1)} %constant_dynamic-slice_fusion), channel_id=1, source_target_pairs={{0,4},{4,8},{8,12},{12,16},{16,20},{20,24},{24,28},{28,32},{32,36}... | collective-permute-start | bytes 688136 | tf_op jit(solution)/shard_map/ppermute | solution.py:19
  24.3 48.6 %collective-permute-start.5 = (bf16[64,4096]{1,0:T(8,128)(2,1)}, bf16[64,4096]{1,0:T(8,128)(2,1)}, u32[]{:S(2)}, u32[]{:S(2)}) collective-permute-start(bf16[64,4096]{1,0:T(8,128)(2,1)} %slice.62), channel_id=1, source_target_pairs={{0,4},{4,8},{8,12},{12,16},{16,20},{20,24},{24,28},{28,32},{32,36}... | collective-permute-start | bytes 1572872 | tf_op jit(solution)/shard_map/ppermute | solution.py:19
  27.0 4.5 %copy-start.17 = (s32[8,2]{0,1:T(2,128)S(1)}, s32[8,2]{0,1:T(2,128)}, u32[]{:S(2)}) copy-start(s32[8,2]{0,1:T(2,128)} %param.15) | copy-start | bytes 196
  27.0 4.5 %copy-start.18 = (s32[8,2]{0,1:T(2,128)S(1)}, s32[8,2]{0,1:T(2,128)}, u32[]{:S(2)}) copy-start(s32[8,2]{0,1:T(2,128)} %param.16) | copy-start | bytes 196
  40.7 14.7 %collective-permute-start.2 = (bf16[2,128,896]{2,1,0:T(8,128)(2,1)}, bf16[2,128,896]{2,1,0:T(8,128)(2,1)S(1)}, u32[]{:S(2)}, u32[]{:S(2)}) collective-permute-start(bf16[2,128,896]{2,1,0:T(8,128)(2,1)} %broadcast_select_fusion.3), channel_id=1, source_target_pairs={{0,1},{1,2},{2,3},{3,0},{4,5},{5,6},{6,7},{7,4},{8,9},{9,10},{10,1... | collective-permute-start | bytes 1376264 | tf_op jit(solution)/shard_map/ppermute | solution.py:24
  45.4 21.1 %collective-permute-start.3 = (bf16[2,128,896]{2,1,0:T(8,128)(2,1)}, bf16[2,128,896]{2,1,0:T(8,128)(2,1)S(1)}, u32[]{:S(2)}, u32[]{:S(2)}) collective-permute-start(bf16[2,128,896]{2,1,0:T(8,128)(2,1)} %broadcast_select_fusion.2), channel_id=1, source_target_pairs={{0,2},{1,3},{2,0},{3,1},{4,6},{5,7},{6,4},{7,5},{8,10},{9,11},{10,... | collective-permute-start | bytes 1376264 | tf_op jit(solution)/shard_map/ppermute | solution.py:24
  51.4 17.6 %collective-permute-start.4 = (bf16[2,128,896]{2,1,0:T(8,128)(2,1)}, bf16[2,128,896]{2,1,0:T(8,128)(2,1)S(1)}, u32[]{:S(2)}, u32[]{:S(2)}) collective-permute-start(bf16[2,128,896]{2,1,0:T(8,128)(2,1)} %broadcast_select_fusion.1), channel_id=1, source_target_pairs={{0,3},{1,0},{2,1},{3,2},{4,7},{5,4},{6,5},{7,6},{8,11},{9,8},{10,9... | collective-permute-start | bytes 1376264 | tf_op jit(solution)/shard_map/ppermute | solution.py:24
  55.5 13.6 %copy-start.14 = (bf16[2,128,896]{2,1,0:T(8,128)(2,1)}, bf16[2,128,896]{2,1,0:T(8,128)(2,1)S(1)}, u32[]{:S(2)}) copy-start(bf16[2,128,896]{2,1,0:T(8,128)(2,1)S(1)} %collective-permute-done.2) | copy-start | bytes 1376260
  66.5 2.5 copy-start.15
  69.0 0.8 copy-start.16
  78.5 5.3 %copy-start.12 = (bf16[4,128,896]{2,1,0:T(8,128)(2,1)S(1)}, bf16[4,128,896]{2,1,0:T(8,128)(2,1)}, u32[]{:S(2)}) copy-start(bf16[4,128,896]{2,1,0:T(8,128)(2,1)} %gather_fusion) | copy-start | bytes 2752516
  79.4 13.2 %all-to-all-start = ((bf16[4,128,448]{1,2,0:T(8,128)(2,1)}), bf16[4,128,448]{1,2,0:T(8,128)(2,1)S(1)}, u32[]{:S(2)}, u32[]{:S(2)}) async-start(bf16[4,128,448]{1,2,0:T(8,128)(2,1)} %bitcast.79), calls=%async_computation | async-start | bytes 917504 | tf_op jit(solution)/shard_map/all_to_all | solution.py:355
  83.8 263.1 %reduce-scatter.9.cloned.1.call-start = ((), (), s32[]{:S(2)}) async-start(), calls=%async_computation.7 | async-start | bytes 4325376
  86.6 0.9 copy-start.5
  93.0 1.4 copy-start.6
  99.7 48.1 %collective-permute-start.8 = (bf16[4,128,896]{2,1,0:T(8,128)(2,1)}, bf16[4,128,896]{2,1,0:T(8,128)(2,1)}, u32[]{:S(2)}, u32[]{:S(2)}) collective-permute-start(bf16[4,128,896]{2,1,0:T(8,128)(2,1)} %encode.1.coded_ref), channel_id=1, source_target_pairs={{0,1},{1,2},{2,3},{3,0},{4,5},{5,6},{6,7},{7,4},{8,9},{9,10},{10,1... | collective-permute-start | bytes 2752520 | tf_op jit(solution)/shard_map/ppermute | solution.py:24
  100.1 54.6 %collective-permute-start.7 = (bf16[4,128,896]{2,1,0:T(8,128)(2,1)}, bf16[4,128,896]{2,1,0:T(8,128)(2,1)}, u32[]{:S(2)}, u32[]{:S(2)}) collective-permute-start(bf16[4,128,896]{2,1,0:T(8,128)(2,1)} %encode.1.coded_ref), channel_id=1, source_target_pairs={{0,3},{1,0},{2,1},{3,2},{4,7},{5,4},{6,5},{7,6},{8,11},{9,8},{10,9... | collective-permute-start | bytes 2752520 | tf_op jit(solution)/shard_map/ppermute | solution.py:24
  102.9 58.7 %collective-permute-start.6 = (bf16[4,128,896]{2,1,0:T(8,128)(2,1)}, bf16[4,128,896]{2,1,0:T(8,128)(2,1)}, u32[]{:S(2)}, u32[]{:S(2)}) collective-permute-start(bf16[4,128,896]{2,1,0:T(8,128)(2,1)} %encode.1.coded_ref), channel_id=1, source_target_pairs={{0,2},{1,3},{2,0},{3,1},{4,6},{5,7},{6,4},{7,5},{8,10},{9,11},{10,... | collective-permute-start | bytes 2752520 | tf_op jit(solution)/shard_map/ppermute | solution.py:24
  127.0 2.2 copy-start.2
  129.2 2.2 copy-start.4
  131.4 9.5 %copy-start.7 = (bf16[896,1024]{1,0:T(8,128)(2,1)S(1)}, bf16[896,1024]{1,0:T(8,128)(2,1)}, u32[]{:S(2)}) copy-start(bf16[896,1024]{1,0:T(8,128)(2,1)} %reshape.295.w_ref) | copy-start | bytes 5505028
  161.6 50.9 %copy-start.3 = (bf16[896,896]{1,0:T(8,128)(2,1)S(1)}, bf16[896,896]{1,0:T(8,128)(2,1)}, u32[]{:S(2)}) copy-start(bf16[896,896]{1,0:T(8,128)(2,1)} %get-tuple-element.53.w_in_ref) | copy-start | bytes 4816900
  168.6 24.8 %collective-permute-start.11 = (bf16[4,128,896]{2,1,0:T(8,128)(2,1)S(1)}, bf16[4,128,896]{2,1,0:T(8,128)(2,1)S(1)}, u32[]{:S(2)}, u32[]{:S(2)}) collective-permute-start(bf16[4,128,896]{2,1,0:T(8,128)(2,1)S(1)} %get-tuple-element.23), channel_id=1, source_target_pairs={{0,2},{1,3},{2,0},{3,1},{4,6},{5,7},{6,4},{7,5},{8,10},{9,11},{10,... | collective-permute-start | bytes 2752520 | tf_op jit(solution)/shard_map/ppermute | solution.py:24
  171.7 40.7 %collective-permute-start.10 = (bf16[4,128,896]{2,1,0:T(8,128)(2,1)S(1)}, bf16[4,128,896]{2,1,0:T(8,128)(2,1)S(1)}, u32[]{:S(2)}, u32[]{:S(2)}) collective-permute-start(bf16[4,128,896]{2,1,0:T(8,128)(2,1)S(1)} %get-tuple-element.22), channel_id=1, source_target_pairs={{0,1},{1,2},{2,3},{3,0},{4,5},{5,6},{6,7},{7,4},{8,9},{9,10},{10,1... | collective-permute-start | bytes 2752520 | tf_op jit(solution)/shard_map/ppermute | solution.py:24
  172.3 40.2 %collective-permute-start.9 = (bf16[4,128,896]{2,1,0:T(8,128)(2,1)S(1)}, bf16[4,128,896]{2,1,0:T(8,128)(2,1)S(1)}, u32[]{:S(2)}, u32[]{:S(2)}) collective-permute-start(bf16[4,128,896]{2,1,0:T(8,128)(2,1)S(1)} %get-tuple-element.21), channel_id=1, source_target_pairs={{0,3},{1,0},{2,1},{3,2},{4,7},{5,4},{6,5},{7,6},{8,11},{9,8},{10,9... | collective-permute-start | bytes 2752520 | tf_op jit(solution)/shard_map/ppermute | solution.py:24
  228.4 0.9 copy-start.8
  229.3 0.7 copy-start.10
  230.0 0.7 copy-start.11
  258.7 167.3 %reduce-scatter.7.cloned.1.call-start = ((), (), s32[]{:S(2)}) async-start(), calls=%async_computation.6 | async-start | bytes 4325376
  271.9 1.2 copy-start.9
  275.1 44.3 %collective-permute-start.16 = (bf16[2,128,896]{2,1,0:T(8,128)(2,1)}, bf16[2,128,896]{2,1,0:T(8,128)(2,1)}, u32[]{:S(2)}, u32[]{:S(2)}) collective-permute-start(bf16[2,128,896]{2,1,0:T(8,128)(2,1)} %get-tuple-element.40), channel_id=1, source_target_pairs={{0,1},{1,2},{2,3},{3,0},{4,5},{5,6},{6,7},{7,4},{8,9},{9,10},{10,1... | collective-permute-start | bytes 1376264 | tf_op jit(solution)/shard_map/ppermute | solution.py:24
  275.7 44.0 %collective-permute-start.17 = (bf16[2,128,896]{2,1,0:T(8,128)(2,1)S(1)}, bf16[2,128,896]{2,1,0:T(8,128)(2,1)}, u32[]{:S(2)}, u32[]{:S(2)}) collective-permute-start(bf16[2,128,896]{2,1,0:T(8,128)(2,1)S(1)} %get-tuple-element.41), channel_id=1, source_target_pairs={{0,2},{1,3},{2,0},{3,1},{4,6},{5,7},{6,4},{7,5},{8,10},{9,11},{10,... | collective-permute-start | bytes 1376264 | tf_op jit(solution)/shard_map/ppermute | solution.py:24
  277.8 41.9 %collective-permute-start.18 = (bf16[2,128,896]{2,1,0:T(8,128)(2,1)S(1)}, bf16[2,128,896]{2,1,0:T(8,128)(2,1)}, u32[]{:S(2)}, u32[]{:S(2)}) collective-permute-start(bf16[2,128,896]{2,1,0:T(8,128)(2,1)S(1)} %get-tuple-element.42), channel_id=1, source_target_pairs={{0,3},{1,0},{2,1},{3,2},{4,7},{5,4},{6,5},{7,6},{8,11},{9,8},{10,9... | collective-permute-start | bytes 1376264 | tf_op jit(solution)/shard_map/ppermute | solution.py:24
  278.7 3.1 collective-permute-start.12
  281.9 2.3 copy-start
  286.9 49.2 %collective-permute-start.13 = (bf16[512,1024]{1,0:T(8,128)(2,1)S(1)}, bf16[512,1024]{1,0:T(8,128)(2,1)}, u32[]{:S(2)}, u32[]{:S(2)}) collective-permute-start(bf16[512,1024]{1,0:T(8,128)(2,1)S(1)} %grad_x_block.4), channel_id=1, source_target_pairs={{0,2},{1,3},{2,0},{3,1},{4,6},{5,7},{6,4},{7,5},{8,10},{9,11},{10,... | collective-permute-start | bytes 3145736 | tf_op jit(solution)/shard_map/ppermute | solution.py:24
  292.9 49.8 %collective-permute-start.14 = (bf16[512,1024]{1,0:T(8,128)(2,1)}, bf16[512,1024]{1,0:T(8,128)(2,1)}, u32[]{:S(2)}, u32[]{:S(2)}) collective-permute-start(bf16[512,1024]{1,0:T(8,128)(2,1)} %grad_x_block.5), channel_id=1, source_target_pairs={{0,1},{1,2},{2,3},{3,0},{4,5},{5,6},{6,7},{7,4},{8,9},{9,10},{10,1... | collective-permute-start | bytes 3145736 | tf_op jit(solution)/shard_map/ppermute | solution.py:24
  319.4 23.7 %collective-permute-start.15 = (bf16[512,1024]{1,0:T(8,128)(2,1)}, bf16[512,1024]{1,0:T(8,128)(2,1)}, u32[]{:S(2)}, u32[]{:S(2)}) collective-permute-start(bf16[512,1024]{1,0:T(8,128)(2,1)} %grad_x_block.6), channel_id=1, source_target_pairs={{0,3},{1,0},{2,1},{3,2},{4,7},{5,4},{6,5},{7,6},{8,11},{9,8},{10,9... | collective-permute-start | bytes 3145736 | tf_op jit(solution)/shard_map/ppermute | solution.py:24
  326.0 4.4 %copy-start.1 = (bf16[4096,448]{1,0:T(8,128)(2,1)S(1)}, bf16[4096,448]{1,0:T(8,128)(2,1)}, u32[]{:S(2)}) copy-start(bf16[4096,448]{1,0:T(8,128)(2,1)} %all-gather.4.cloned.1.call-done.wc_ref) | copy-start | bytes 11010052
  329.1 4.4 %collective-permute-start.19 = (bf16[1,128,896]{2,0,1:T(2,128)(2,1)S(1)}, bf16[1,128,896]{2,0,1:T(2,128)(2,1)S(1)}, u32[]{:S(2)}, u32[]{:S(2)}) collective-permute-start(bf16[1,128,896]{2,0,1:T(2,128)(2,1)S(1)} %slice.94), channel_id=1, source_target_pairs={{4,0},{8,4},{12,8},{16,12},{20,16},{24,20},{28,24},{32,28},{36,32}... | collective-permute-start | bytes 688136 | tf_op jit(solution)/shard_map/ppermute | solution.py:19
Sparse Core Ops, SparseCore 0:
  10.8 49.7 all-gather.3
  62.9 57.2 all-gather.5
  258.8 80.6 reduce-scatter.8
  344.0 81.8 reduce-scatter.6
